TPU v7x, 32 devices: a whole 2x2x4 slice. The times are simulated.
32 devices in a mesh: space: 16 (over z, x, core), rep: 2 (over y).
Axes of the slice: x: 2, y: 2, z: 4, core: 2. Of those that a mesh axis runs over, the one named last changes fastest.
Arguments:
- input_field: bfloat16 [2, 128, 128, 32, 128], P('rep', 'space'), may hold values from -6 to 6
- cotangent: bfloat16 [2, 128, 128, 32, 128], P('rep', 'space'), may hold values from -6 to 6
- mode_weight: float32 [256, 24, 2048], P('space', 'rep'), may hold values from -0.004 to 0.004
- first_moment: float32 [256, 24, 2048], P('space', 'rep'), may hold values from -3 to 3
- second_moment: float32 [256, 24, 2048], P('space', 'rep'), may hold values from 0.001 to 0.05
Outputs:
- layer_output: bfloat16 [2, 128, 128, 32, 128], P('rep', 'space')
- input_gradient: bfloat16 [2, 128, 128, 32, 128], P('rep', 'space')
- new_weight: float32 [256, 24, 2048], P('space', 'rep')
- new_first: float32 [256, 24, 2048], P('space', 'rep')
- new_second: float32 [256, 24, 2048], P('space', 'rep')
All inputs are finite; a program needn't handle non-finite values.
Results may differ from a plain program's by a relative error of at most 0.019.
Values may be sent and summed in bfloat16 or wider, within the bound.
A program may use at most 128 MiB of HBM per device.

v0:
```python
import functools
import math

import jax
import jax.numpy as jnp
import numpy as np
from jax import lax
from jax.experimental import pallas as pl
from jax.experimental.pallas import tpu as pltpu
from jax.sharding import PartitionSpec as P

C = 32
NX = 128
NY = 128
NZ = 128
KX = 24
KY = 16
KZ = 16
STEP = 10
CC = C * C
LANES = 4 * C
ROWS = 16

beta_one = 0.9
beta_two = 0.999
learning_rate = 0.001
epsilon = 1e-08
norm_scale = 1.0 / math.sqrt(NX * NY * NZ)

f32 = jnp.float32
bf16 = jnp.bfloat16


def kept_frequency(count, length):
    number = np.arange(count)
    return np.where(number < count // 2, number, length - count + number)


def wave_tables(frequency, length):
    product = frequency[:, None] * np.arange(length)[None, :] % length
    radians = product * (2.0 * math.pi / length)
    return np.cos(radians).astype(np.float32), np.sin(radians).astype(np.float32)


def constant(array):
    return jnp.asarray(np.asarray(array, np.float32), dtype=bf16)


def depth_tables():
    cosine, sine = wave_tables(np.arange(KZ), NZ)
    weighting = np.where(np.arange(KZ) == 0, 1.0, 2.0)[:, None]
    plain = np.concatenate([cosine, -sine], axis=0)
    doubled = np.concatenate([weighting * cosine, -weighting * sine], axis=0)
    return constant(plain), constant(doubled)


def row_table():
    cosine, sine = wave_tables(kept_frequency(KY, NY), NY)
    return constant(np.stack([np.stack([cosine, sine]), np.stack([-sine, cosine])]))


def plane_table(reps):
    own = KX // reps
    cosine, sine = wave_tables(kept_frequency(KX, NX), NX)
    tables = np.zeros((2, reps, ROWS, NX), np.float32)
    tables[0, :, :own] = cosine.reshape(reps, own, NX)
    tables[1, :, :own] = sine.reshape(reps, own, NX)
    return tables.reshape(2, reps * ROWS, NX)


def rotation():
    table = np.zeros((LANES, LANES), np.float32)
    for field in range(2):
        for c in range(C):
            real, imag = field * 2 * C + c, field * 2 * C + C + c
            table[imag, real] = 1.0
            table[real, imag] = -1.0
    return constant(table)


def spread_tables():
    table = np.zeros((LANES, 4, CC), np.float32)
    pair = np.arange(CC)
    for part in range(2):
        table[part * C + pair // C, part, pair] = 1.0
        table[2 * C + part * C + pair % C, 2 + part, pair] = 1.0
    return constant(table.reshape(LANES, 4 * CC))


def gather_tables():
    table = np.zeros((4, CC, LANES), np.float32)
    pair = np.arange(CC)
    for part in range(2):
        table[part, pair, part * C + pair % C] = 1.0
        table[2 + part, pair, 2 * C + part * C + pair // C] = 1.0
    return constant(table)


def depth_kernel(field_ref, grad_ref, field_table, grad_table, out_ref):
    for k, (ref, table) in enumerate(((field_ref, field_table), (grad_ref, grad_table))):
        out_ref[k, 0] = lax.dot_general(
            table[...], ref[0], (((1,), (1,)), ((), ())), preferred_element_type=f32
        ).astype(bf16)


def depth_forward(input_field, cotangent):
    plain, doubled = depth_tables()
    planes = input_field.shape[1]
    rows = NY * C
    block = pl.BlockSpec((1, rows, NZ), lambda i: (i, 0, 0))
    table = pl.BlockSpec((2 * KZ, NZ), lambda i: (0, 0))
    return pl.pallas_call(
        depth_kernel,
        grid=(planes,),
        in_specs=[block, block, table, table],
        out_specs=pl.BlockSpec((2, 1, 2 * KZ, rows), lambda i: (0, i, 0, 0)),
        out_shape=jax.ShapeDtypeStruct((2, planes, 2 * KZ, rows), bf16),
        compiler_params=pltpu.CompilerParams(vmem_limit_bytes=40 * 2**20),
        name="depth_forward",
    )(input_field.reshape(planes, rows, NZ), cotangent.reshape(planes, rows, NZ), plain, doubled)


def grid_kernel(rows_ref, output_table, grad_table, output_ref, grad_ref):
    for k, (ref, table) in enumerate(((output_ref, output_table), (grad_ref, grad_table))):
        ref[0] = (
            lax.dot_general(
                rows_ref[k, 0], table[...], (((0,), (0,)), ((), ())), preferred_element_type=f32
            )
            * norm_scale
        ).astype(bf16)


def depth_inverse(rows_in):
    plain, doubled = depth_tables()
    planes, rows = rows_in.shape[1], NY * C
    block = pl.BlockSpec((1, rows, NZ), lambda i: (i, 0, 0))
    table = pl.BlockSpec((2 * KZ, NZ), lambda i: (0, 0))
    outputs = pl.pallas_call(
        grid_kernel,
        grid=(planes,),
        in_specs=[pl.BlockSpec((2, 1, 2 * KZ, rows), lambda i: (0, i, 0, 0)), table, table],
        out_specs=[block, block],
        out_shape=[jax.ShapeDtypeStruct((planes, rows, NZ), bf16)] * 2,
        compiler_params=pltpu.CompilerParams(vmem_limit_bytes=40 * 2**20),
        name="depth_inverse",
    )(rows_in, doubled, plain)
    return [value.reshape(1, planes, NY, C, NZ) for value in outputs]


def modes_kernel(reps, columns_ref, table_ref, turn_ref, out_ref):
    for m in range(columns_ref.shape[0]):
        columns = columns_ref[m]
        turned = jnp.dot(columns, turn_ref[...], preferred_element_type=f32).astype(bf16)
        both = jnp.concatenate([columns, turned], axis=0)
        modes = jnp.dot(table_ref[...], both, preferred_element_type=f32) * norm_scale
        modes = modes.astype(bf16)
        for r in range(reps):
            out_ref[r, m] = modes[r * ROWS : (r + 1) * ROWS]


def grid_modes(columns, reps):
    cosine, sine = plane_table(reps)
    owned = columns.shape[0]
    return pl.pallas_call(
        functools.partial(modes_kernel, reps),
        out_shape=jax.ShapeDtypeStruct((reps, owned, ROWS, LANES), bf16),
        compiler_params=pltpu.CompilerParams(vmem_limit_bytes=40 * 2**20),
        name="grid_modes",
    )(columns, constant(np.concatenate([cosine, sine], axis=1)), rotation())


def planes_kernel(reps, modes_ref, table_ref, turn_ref, out_ref):
    for m in range(out_ref.shape[0]):
        modes = jnp.concatenate([modes_ref[r, m] for r in range(reps)], axis=0)
        turned = jnp.dot(modes, turn_ref[...], preferred_element_type=f32).astype(bf16)
        both = jnp.concatenate([modes, turned], axis=0)
        out_ref[m] = jnp.dot(table_ref[...], both, preferred_element_type=f32).astype(bf16)


def mode_planes(modes, reps):
    cosine, sine = plane_table(reps)
    owned = modes.shape[1]
    return pl.pallas_call(
        functools.partial(planes_kernel, reps),
        out_shape=jax.ShapeDtypeStruct((owned, NX, LANES), bf16),
        compiler_params=pltpu.CompilerParams(vmem_limit_bytes=40 * 2**20),
        name="mode_planes",
    )(modes, constant(np.concatenate([cosine.T, -sine.T], axis=1)), rotation())


def mix_kernel(
    modes_ref, weight_ref, first_ref, second_ref, spread_ref, gather_ref,
    mixed_ref, new_weight_ref, new_first_ref, new_second_ref, padded,
):
    samples, owned = modes_ref.shape[0], modes_ref.shape[1]
    own = weight_ref.shape[1]
    rows = owned * ROWS
    padded[...] = jnp.zeros_like(padded)
    padded[:, :own] = weight_ref[...].astype(bf16).astype(f32)
    weight = padded[...].reshape(rows, 2 * CC)
    real, imag = weight[:, :CC], weight[:, CC:]
    grad_real = jnp.zeros((rows, CC), f32)
    grad_imag = jnp.zeros((rows, CC), f32)
    for b in range(samples):
        modes = modes_ref[b].reshape(rows, LANES)
        ur, ui, gr, gi = [
            jnp.dot(modes, spread_ref[:, k * CC : (k + 1) * CC], preferred_element_type=f32)
            for k in range(4)
        ]
        terms = (
            ur * real - ui * imag,
            ur * imag + ui * real,
            gr * real + gi * imag,
            gi * real - gr * imag,
        )
        mixed = jnp.zeros((rows, LANES), f32)
        for k in range(4):
            mixed += jnp.dot(terms[k].astype(bf16), gather_ref[k], preferred_element_type=f32)
        mixed_ref[b] = mixed.astype(bf16).reshape(owned, ROWS, LANES)
        grad_real += ur * gr + ui * gi
        grad_imag += ur * gi - ui * gr
    for part, gradient in enumerate((grad_real, grad_imag)):
        lanes = slice(part * CC, (part + 1) * CC)
        gradient = gradient.reshape(owned, ROWS, CC)[:, :own]
        new_first = beta_one * first_ref[:, :, lanes] + (1.0 - beta_one) * gradient
        new_second = (
            beta_two * second_ref[:, :, lanes] + (1.0 - beta_two) * gradient * gradient
        )
        corrected = (new_first / (1.0 - beta_one**STEP)) / (
            jnp.sqrt(new_second / (1.0 - beta_two**STEP)) + epsilon
        )
        new_first_ref[:, :, lanes] = new_first
        new_second_ref[:, :, lanes] = new_second
        new_weight_ref[:, :, lanes] = weight_ref[:, :, lanes] - learning_rate * corrected


def mix_and_update(modes, mode_weight, first_moment, second_moment):
    samples, owned = modes.shape[0], modes.shape[1]
    own = mode_weight.shape[1]
    step = min(owned, 4)
    weights = pl.BlockSpec((step, own, 2 * CC), lambda i: (i, 0, 0))
    blocks = pl.BlockSpec((samples, step, ROWS, LANES), lambda i: (0, i, 0, 0))
    like_weight = jax.ShapeDtypeStruct(mode_weight.shape, f32)
    return pl.pallas_call(
        mix_kernel,
        grid=(owned // step,),
        in_specs=[
            blocks,
            weights,
            weights,
            weights,
            pl.BlockSpec((LANES, 4 * CC), lambda i: (0, 0)),
            pl.BlockSpec((4, CC, LANES), lambda i: (0, 0, 0)),
        ],
        out_specs=[blocks, weights, weights, weights],
        out_shape=[jax.ShapeDtypeStruct(modes.shape, bf16), like_weight, like_weight, like_weight],
        scratch_shapes=[pltpu.VMEM((step, ROWS, 2 * CC), f32)],
        compiler_params=pltpu.CompilerParams(vmem_limit_bytes=48 * 2**20),
        name="mix_and_update",
    )(modes, mode_weight, first_moment, second_moment, spread_tables(), gather_tables())


def local(reps, input_field, cotangent, mode_weight, first_moment, second_moment):
    planes = input_field.shape[1]
    rows = row_table()
    depth = depth_forward(input_field, cotangent)
    depth = depth.reshape(2, planes, 2, KZ, NY, C)
    slabs = jnp.einsum("rpqy,fxpsyc->qsxfrc", rows, depth, preferred_element_type=f32)
    slabs = slabs.astype(bf16).reshape(KY * KZ, planes, LANES)
    columns = lax.all_to_all(slabs, "space", split_axis=0, concat_axis=1, tiled=True)
    modes = grid_modes(columns, reps)
    modes = lax.all_to_all(modes, "rep", split_axis=0, concat_axis=0, tiled=True)
    mixed, new_weight, new_first, new_second = mix_and_update(
        modes, mode_weight, first_moment, second_moment
    )
    mixed = lax.all_to_all(mixed, "rep", split_axis=0, concat_axis=0, tiled=True)
    columns = mode_planes(mixed, reps)
    slabs = lax.all_to_all(columns, "space", split_axis=1, concat_axis=0, tiled=True)
    slabs = slabs.reshape(KY, KZ, planes, 2, 2, C)
    grid_rows = jnp.einsum("rpqy,qsxfrc->fxpsyc", rows, slabs, preferred_element_type=f32)
    grid_rows = grid_rows.astype(bf16).reshape(2, planes, 2 * KZ, NY * C)
    layer_output, input_gradient = depth_inverse(grid_rows)
    return (layer_output, input_gradient, new_weight, new_first, new_second)


def solution(mesh):
    grids = P("rep", "space", None, None, None)
    weights = P("space", "rep", None)
    return jax.shard_map(
        functools.partial(local, mesh.shape["rep"]),
        mesh=mesh,
        in_specs=(grids, grids, weights, weights, weights),
        out_specs=(grids, grids, weights, weights, weights),
        check_vma=False,
    )
```

profile of v0, /device:TPU:0, one launch (start us, length us, event | category | flops | bytes accessed | tf_op | source)
XLA Modules:
  0.0 170.9 jit_solution(17330042272054407865)
XLA Ops:
  0.6 0.0 copy-start.2
  0.6 3.4 %copy-done.2 = bf16[1,8,128,32,128]{4,3,2,1,0:T(8,128)(2,1)S(1)} copy-done((bf16[1,8,128,32,128]{4,3,2,1,0:T(8,128)(2,1)S(1)}, bf16[1,8,128,32,128]{4,3,2,1,0:T(8,128)(2,1)}, u32[]{:S(2)}) %copy-start.2) | copy-done | bytes 8388632
  4.0 0.0 copy-start.6
  4.0 0.7 copy-done.6
  4.7 0.0 copy-start.8
  4.7 0.7 copy-done.8
  5.4 9.3 %depth_forward.1 = bf16[2,8,32,4096]{3,2,1,0:T(8,128)(2,1)S(1)} custom-call(bf16[8,4096,128]{2,1,0:T(8,128)(2,1)S(1)} %bitcast.45, bf16[8,4096,128]{2,1,0:T(8,128)(2,1)} %bitcast.48, bf16[32,128]{1,0:T(8,128)(2,1)S(1)} %copy-done.8, bf16[32,128]{1,0:T(8,128)(2,1)S(1)} %copy-done.6), custom_call_target="tpu_custom_call" | custom-call | tf_op jit(solution)/shard_map/depth_forward/pallas_call | solution.py:112
  14.7 0.0 copy-start.1
  14.8 2.0 %copy-done.1 = bf16[2,8,32,4096]{3,2,1,0:T(8,128)(2,1)} copy-done((bf16[2,8,32,4096]{3,2,1,0:T(8,128)(2,1)}, bf16[2,8,32,4096]{3,2,1,0:T(8,128)(2,1)S(1)}, u32[]{:S(2)}) %copy-start.1) | copy-done | bytes 4194328
  16.8 0.0 copy-start.17
  16.8 17.2 %reshape.37 = bf16[2,8,2,16,128,32]{5,4,3,2,1,0:T(8,128)(2,1)} reshape(bf16[2,8,32,4096]{3,2,1,0:T(8,128)(2,1)} %copy-done.1) | data formatting | bytes 8388608 | tf_op jit(solution)/shard_map/reshape | solution.py:267
  34.0 0.0 copy-done.17
  34.0 7.3 %fusion.6 = bf16[16,16,8,2,2,32]{5,0,4,1,2,3:T(8,128)(2,1)S(1)} fusion(bf16[2,2,16,128,1,1,1]{3,2,1,0,6,5,4:T(8,128)(2,1)S(1)} %copy-done.17, bf16[2,8,2,16,128,32]{5,4,3,2,1,0:T(8,128)(2,1)} %reshape.37), kind=kOutput, calls=%fused_computation.6 | convolution fusion | flops 134479872 | bytes 4734976 | tf_op jit(solution)/shard_map/rpqy,fxpsyc->qsxfrc/dot_general | solution.py:268
  41.3 2.0 %copy.44 = bf16[16,16,8,2,2,32]{5,4,3,2,1,0:T(2,128)(2,1)S(1)} copy(bf16[16,16,8,2,2,32]{5,0,4,1,2,3:T(8,128)(2,1)S(1)} %fusion.6) | data formatting | bytes 1048576 | tf_op jit(solution)/shard_map/convert_element_type | solution.py:269
  43.3 0.0 copy-start.5
  43.3 0.0 copy-start.11
  43.3 1.1 reshape.38
  44.4 21.6 %all_to_all.43 = bf16[256,8,128]{2,1,0:T(8,128)(2,1)S(1)} all-to-all(bf16[256,8,128]{2,1,0:T(8,128)(2,1)S(1)} %reshape.38), channel_id=1, replica_groups=mesh['space'=16,'rep'=2] {'space'}, dimensions={0} | all-to-all | bytes 1048576 | tf_op jit(solution)/shard_map/all_to_all | solution.py:270
  66.0 0.1 copy.80
  66.1 0.0 copy-done.5
  66.1 0.0 copy-done.11
  66.2 1.2 grid_modes.1
  67.3 0.0 copy-start.14
  67.3 3.5 %all-to-all-start.1 = ((bf16[2,16,16,128]{3,2,1,0:T(8,128)(2,1)}), bf16[2,16,16,128]{3,2,1,0:T(8,128)(2,1)S(1)}, u32[]{:S(2)}, u32[]{:S(2)}) async-start(bf16[2,16,16,128]{3,2,1,0:T(8,128)(2,1)} %grid_modes.1), calls=%async_computation.1 | async-start | bytes 262144 | tf_op jit(solution)/shard_map/all_to_all | solution.py:272
  70.9 3.7 %copy.46.weight_ref = f32[16,12,2048]{2,1,0:T(8,128)} copy(f32[16,12,2048]{2,0,1:T(8,128)} %param.18) | data formatting | bytes 3145728 | tf_op args[2]
  74.5 0.0 copy-done.14
  74.5 0.0 copy-start.15
  74.5 2.2 %copy.47.first_ref = f32[16,12,2048]{2,1,0:T(8,128)} copy(f32[16,12,2048]{2,0,1:T(8,128)S(1)} %copy-done.14) | data formatting | bytes 3145728 | tf_op args[3]
  76.8 0.0 copy-done.15
  76.8 0.0 copy-start.3
  76.8 2.3 %copy.48.second_ref = f32[16,12,2048]{2,1,0:T(8,128)} copy(f32[16,12,2048]{2,0,1:T(8,128)S(1)} %copy-done.15) | data formatting | bytes 3145728 | tf_op args[4]
  79.0 0.0 all-to-all-done.1.modes_ref
  79.0 0.0 copy-done.3
  79.1 0.0 copy-start.4
  79.1 1.2 copy-done.4
  80.3 0.0 copy-start.10
  80.3 8.7 %mix_and_update.1 = (bf16[2,16,16,128]{3,2,1,0:T(8,128)(2,1)S(1)}, f32[16,12,2048]{2,1,0:T(8,128)S(1)}, f32[16,12,2048]{2,1,0:T(8,128)}, f32[16,12,2048]{2,1,0:T(8,128)}) custom-call(bf16[2,16,16,128]{3,2,1,0:T(8,128)(2,1)S(1)} %all-to-all-done.1.modes_ref, f32[16,12,2048]{2,1,0:T(8,128)} %copy.46.weight_ref, f32[16,12,2048]{2,1,0:T(8,128)} %copy.47.first_ref, ...), custom_call_target="tpu_custom_call" | custom-call | tf_op jit(solution)/shard_map/mix_and_update/pallas_call | solution.py:244
  89.0 7.5 %all_to_all.44.modes_ref = bf16[2,16,16,128]{3,2,1,0:T(8,128)(2,1)S(1)} all-to-all(bf16[2,16,16,128]{3,2,1,0:T(8,128)(2,1)S(1)} %get-tuple-element.11), channel_id=1, replica_groups=mesh['space'=16,'rep'=2] {'rep'}, dimensions={0} | all-to-all | bytes 262144 | tf_op jit(solution)/shard_map/all_to_all | solution.py:276
  96.5 0.0 copy-done.10
  96.5 2.3 %mode_planes.1 = bf16[16,128,128]{2,1,0:T(8,128)(2,1)S(1)} custom-call(bf16[2,16,16,128]{3,2,1,0:T(8,128)(2,1)S(1)} %all_to_all.44.modes_ref, bf16[128,64]{1,0:T(8,128)(2,1)S(1)} %copy-done.10, bf16[128,128]{1,0:T(8,128)(2,1)S(1)} %copy-done.5), custom_call_target="tpu_custom_call" | custom-call | tf_op jit(solution)/shard_map/mode_planes/pallas_call | solution.py:183
  98.8 1.1 copy.49
  100.0 4.1 %all-to-all-start.3 = ((bf16[16,128,128]{2,0,1:T(8,128)(2,1)}), bf16[16,128,128]{2,0,1:T(8,128)(2,1)S(1)}, u32[]{:S(2)}, u32[]{:S(2)}) async-start(bf16[16,128,128]{2,0,1:T(8,128)(2,1)} %copy.49), calls=%async_computation.3 | async-start | bytes 1048576 | tf_op jit(solution)/shard_map/all_to_all | solution.py:278
  104.1 0.0 copy-start.13
  104.1 2.1 %copy.54 = f32[16,12,2048]{2,0,1:T(8,128)} copy(f32[16,12,2048]{2,1,0:T(8,128)S(1)} %get-tuple-element.29) | data formatting | bytes 3145728
  106.1 0.0 copy-start.12
  106.1 0.0 copy-done.13
  106.1 2.1 %copy.55 = f32[16,12,2048]{2,0,1:T(8,128)} copy(f32[16,12,2048]{2,1,0:T(8,128)S(1)} %copy-done.13) | data formatting | bytes 3145728
  108.2 0.0 copy-done.12
  108.2 2.1 %copy.56 = f32[16,12,2048]{2,0,1:T(8,128)} copy(f32[16,12,2048]{2,1,0:T(8,128)S(1)} %copy-done.12) | data formatting | bytes 3145728
  110.3 0.0 copy-start.16
  110.3 8.3 %all-to-all-done.3 = bf16[16,128,128]{2,0,1:T(8,128)(2,1)S(1)} async-done(((bf16[16,128,128]{2,0,1:T(8,128)(2,1)}), bf16[16,128,128]{2,0,1:T(8,128)(2,1)S(1)}, u32[]{:S(2)}, u32[]{:S(2)}) %all-to-all-start.3) | async-done | bytes 524320 | tf_op jit(solution)/shard_map/all_to_all | solution.py:278
  118.5 0.1 copy.79
  118.7 0.9 reshape.39
  119.5 0.0 copy-done.16
  119.5 3.8 %fusion.2 = bf16[2,8,2,16,128,32]{4,5,2,0,1,3:T(8,128)(2,1)} fusion(bf16[2,2,16,128,1,1,1]{3,2,0,1,6,5,4:T(8,128)(2,1)S(1)} %copy-done.16, bf16[16,16,8,2,2,32,1]{5,4,3,2,1,0,6:T(2,128)(2,1)S(1)} %bitcast.47), kind=kOutput, calls=%fused_computation.3 | convolution fusion | flops 136314880 | bytes 4734976 | tf_op jit(solution)/shard_map/rpqy,qsxfrc->fxpsyc/dot_general | solution.py:280
  123.4 14.4 %copy.53 = bf16[2,8,2,16,128,32]{5,4,3,2,1,0:T(8,128)(2,1)} copy(bf16[2,8,2,16,128,32]{4,5,2,0,1,3:T(8,128)(2,1)} %fusion.2) | data formatting | bytes 8388608 | tf_op jit(solution)/shard_map/convert_element_type | solution.py:281
  137.8 0.0 copy-start.7
  137.8 0.0 copy-start.9
  137.8 21.7 %reshape.40.rows_ref = bf16[2,8,32,4096]{3,2,1,0:T(8,128)(2,1)} reshape(bf16[2,8,2,16,128,32]{5,4,3,2,1,0:T(8,128)(2,1)} %copy.53) | data formatting | bytes 8388608 | tf_op jit(solution)/shard_map/reshape | solution.py:281
  159.5 0.0 copy-done.7
  159.5 0.0 copy-done.9
  159.5 0.0 copy-start
  159.5 2.2 %copy-done = bf16[2,8,32,4096]{3,2,1,0:T(8,128)(2,1)S(1)} copy-done((bf16[2,8,32,4096]{3,2,1,0:T(8,128)(2,1)S(1)}, bf16[2,8,32,4096]{3,2,1,0:T(8,128)(2,1)}, u32[]{:S(2)}) %copy-start) | copy-done | bytes 4194328
  161.7 9.2 %depth_inverse.1 = (bf16[8,4096,128]{2,1,0:T(8,128)(2,1)}, bf16[8,4096,128]{2,1,0:T(8,128)(2,1)}) custom-call(bf16[2,8,32,4096]{3,2,1,0:T(8,128)(2,1)S(1)} %copy-done, bf16[32,128]{1,0:T(8,128)(2,1)S(1)} %copy-done.7, bf16[32,128]{1,0:T(8,128)(2,1)S(1)} %copy-done.9), custom_call_target="tpu_custom_call" | custom-call | tf_op jit(solution)/shard_map/depth_inverse/pallas_call | solution.py:138
Async XLA Ops:
  0.6 3.4 %copy-start.2 = (bf16[1,8,128,32,128]{4,3,2,1,0:T(8,128)(2,1)S(1)}, bf16[1,8,128,32,128]{4,3,2,1,0:T(8,128)(2,1)}, u32[]{:S(2)}) copy-start(bf16[1,8,128,32,128]{4,3,2,1,0:T(8,128)(2,1)} %param.16) | copy-start | bytes 25165828
  4.0 0.7 copy-start.6
  4.7 0.7 copy-start.8
  14.7 2.0 %copy-start.1 = (bf16[2,8,32,4096]{3,2,1,0:T(8,128)(2,1)}, bf16[2,8,32,4096]{3,2,1,0:T(8,128)(2,1)S(1)}, u32[]{:S(2)}) copy-start(bf16[2,8,32,4096]{3,2,1,0:T(8,128)(2,1)S(1)} %depth_forward.1) | copy-start | bytes 12582916
  16.8 17.2 %copy-start.17 = (bf16[2,2,16,128,1,1,1]{3,2,1,0,6,5,4:T(8,128)(2,1)S(1)}, bf16[2,2,16,128,1,1,1]{3,2,1,0,6,5,4:T(8,128)(2,1)}, u32[]{:S(2)}) copy-start(bf16[2,2,16,128,1,1,1]{3,2,1,0,6,5,4:T(8,128)(2,1)} %constant.26) | copy-start | bytes 49156
  43.3 22.9 %copy-start.5 = (bf16[128,128]{1,0:T(8,128)(2,1)S(1)}, bf16[128,128]{1,0:T(8,128)(2,1)}, u32[]{:S(2)}) copy-start(bf16[128,128]{1,0:T(8,128)(2,1)} %constant.20.clone.turn_ref) | copy-start | bytes 98308
  43.3 22.9 %copy-start.11 = (bf16[32,256]{1,0:T(8,128)(2,1)S(1)}, bf16[32,256]{1,0:T(8,128)(2,1)}, u32[]{:S(2)}) copy-start(bf16[32,256]{1,0:T(8,128)(2,1)} %constant.19.clone.table_ref) | copy-start | bytes 49156
  67.3 7.2 %copy-start.14 = (f32[16,12,2048]{2,0,1:T(8,128)S(1)}, f32[16,12,2048]{2,0,1:T(8,128)}, u32[]{:S(2)}) copy-start(f32[16,12,2048]{2,0,1:T(8,128)} %param.19) | copy-start | bytes 4718596
  67.3 11.7 %all-to-all-start.1 = ((bf16[2,16,16,128]{3,2,1,0:T(8,128)(2,1)}), bf16[2,16,16,128]{3,2,1,0:T(8,128)(2,1)S(1)}, u32[]{:S(2)}, u32[]{:S(2)}) async-start(bf16[2,16,16,128]{3,2,1,0:T(8,128)(2,1)} %grid_modes.1), calls=%async_computation.1 | async-start | bytes 262144 | tf_op jit(solution)/shard_map/all_to_all | solution.py:272
  74.5 2.3 %copy-start.15 = (f32[16,12,2048]{2,0,1:T(8,128)S(1)}, f32[16,12,2048]{2,0,1:T(8,128)}, u32[]{:S(2)}) copy-start(f32[16,12,2048]{2,0,1:T(8,128)} %param.20) | copy-start | bytes 4718596
  76.8 2.3 %copy-start.3 = (bf16[4,1024,128]{2,1,0:T(8,128)(2,1)S(1)}, bf16[4,1024,128]{2,1,0:T(8,128)(2,1)}, u32[]{:S(2)}) copy-start(bf16[4,1024,128]{2,1,0:T(8,128)(2,1)} %constant.22.clone.gather_ref) | copy-start | bytes 3145732
  79.1 1.2 copy-start.4
  80.3 16.2 %copy-start.10 = (bf16[128,64]{1,0:T(8,128)(2,1)S(1)}, bf16[128,64]{1,0:T(8,128)(2,1)}, u32[]{:S(2)}) copy-start(bf16[128,64]{1,0:T(8,128)(2,1)} %constant.23.clone.table_ref) | copy-start | bytes 49156
  100.0 18.6 %all-to-all-start.3 = ((bf16[16,128,128]{2,0,1:T(8,128)(2,1)}), bf16[16,128,128]{2,0,1:T(8,128)(2,1)S(1)}, u32[]{:S(2)}, u32[]{:S(2)}) async-start(bf16[16,128,128]{2,0,1:T(8,128)(2,1)} %copy.49), calls=%async_computation.3 | async-start | bytes 1048576 | tf_op jit(solution)/shard_map/all_to_all | solution.py:278
  104.1 2.1 %copy-start.13 = (f32[16,12,2048]{2,1,0:T(8,128)S(1)}, f32[16,12,2048]{2,1,0:T(8,128)}, u32[]{:S(2)}) copy-start(f32[16,12,2048]{2,1,0:T(8,128)} %get-tuple-element.30) | copy-start | bytes 4718596
  106.1 2.1 %copy-start.12 = (f32[16,12,2048]{2,1,0:T(8,128)S(1)}, f32[16,12,2048]{2,1,0:T(8,128)}, u32[]{:S(2)}) copy-start(f32[16,12,2048]{2,1,0:T(8,128)} %get-tuple-element.31) | copy-start | bytes 4718596
  110.3 9.3 %copy-start.16 = (bf16[2,2,16,128,1,1,1]{3,2,0,1,6,5,4:T(8,128)(2,1)S(1)}, bf16[2,2,16,128,1,1,1]{3,2,0,1,6,5,4:T(8,128)(2,1)}, u32[]{:S(2)}) copy-start(bf16[2,2,16,128,1,1,1]{3,2,0,1,6,5,4:T(8,128)(2,1)} %constant.27) | copy-start | bytes 49156
  137.8 21.7 %copy-start.7 = (bf16[32,128]{1,0:T(8,128)(2,1)S(1)}, bf16[32,128]{1,0:T(8,128)(2,1)}, u32[]{:S(2)}) copy-start(bf16[32,128]{1,0:T(8,128)(2,1)} %constant.18.clone.grad_table.output_table) | copy-start | bytes 24580
  137.8 21.7 %copy-start.9 = (bf16[32,128]{1,0:T(8,128)(2,1)S(1)}, bf16[32,128]{1,0:T(8,128)(2,1)}, u32[]{:S(2)}) copy-start(bf16[32,128]{1,0:T(8,128)(2,1)} %constant.17.clone.field_table.grad_table) | copy-start | bytes 24580
  159.5 2.2 %copy-start = (bf16[2,8,32,4096]{3,2,1,0:T(8,128)(2,1)S(1)}, bf16[2,8,32,4096]{3,2,1,0:T(8,128)(2,1)}, u32[]{:S(2)}) copy-start(bf16[2,8,32,4096]{3,2,1,0:T(8,128)(2,1)} %reshape.40.rows_ref) | copy-start | bytes 12582916
where the time goes:
time: 173 us; the launch traced here: 171 us
  local copies, waits for them, and re-layouts  83.3 us (48%)
  Pallas kernels  30.7 us (18%)
  blocking collectives  29.2 us (17%)
  matrix products  11.1 us (6%)
  waiting for transfers between devices  8.27 us (5%)
  starting transfers between devices  7.61 us (4%)
    unnamed x42, local copies, waits for them, and re-layouts  24.6 us
    reshape x1, local copies, waits for them, and re-layouts, local(): grid_rows = grid_rows.astype(bf16).reshape(2, planes, 2 * KZ, NY * C)  21.7 us
    all_to_all x1, blocking collectives, local(): lax.all_to_all(slabs, 'space', split_axis=0, concat_axis=1, tiled=True)  21.6 us
    reshape x1, local copies, waits for them, and re-layouts, local(): depth = depth.reshape(2, planes, 2, KZ, NY, C)  17.2 us
    convert_element_type x1, local copies, waits for them, and re-layouts, local(): grid_rows = grid_rows.astype(bf16).reshape(2, planes, 2 * KZ, NY * C)  14.4 us
    pallas_call x1, Pallas kernels, depth_forward(): pl.pallas_call(depth_kernel, grid=(planes,), in_specs=[block, block, tabl...  9.33 us
    pallas_call x1, Pallas kernels, depth_inverse(): pl.pallas_call(grid_kernel, grid=(planes,), in_specs=[pl.BlockSpec((2, 1,...  9.18 us
    pallas_call x1, Pallas kernels, mix_and_update(): pl.pallas_call(mix_kernel, grid=(owned // step,), in_specs=[blocks, weigh...  8.69 us
  transfers between devices with their start and end apart: 2, of which 1 were waited for; matrix products, arithmetic and copies ran while one was open for 8% of the time, Pallas kernels for 0%

commit v1 on v0

--- a/solution.py
+++ b/solution.py
@@ -54,9 +54,9 @@
     return constant(plain), constant(doubled)
 
 
-def row_table():
+def row_tables():
     cosine, sine = wave_tables(kept_frequency(KY, NY), NY)
-    return constant(np.stack([np.stack([cosine, sine]), np.stack([-sine, cosine])]))
+    return constant(cosine), constant(sine)
 
 
 def plane_table(reps):
@@ -97,10 +97,19 @@
 
 
 def depth_kernel(field_ref, grad_ref, field_table, grad_table, out_ref):
-    for k, (ref, table) in enumerate(((field_ref, field_table), (grad_ref, grad_table))):
-        out_ref[k, 0] = lax.dot_general(
-            table[...], ref[0], (((1,), (1,)), ((), ())), preferred_element_type=f32
-        ).astype(bf16)
+    out_ref[0] = (
+        jnp.dot(field_ref[0], field_table[...], preferred_element_type=f32)
+        + jnp.dot(grad_ref[0], grad_table[...], preferred_element_type=f32)
+    ).astype(bf16)
+
+
+def lane_table(table, field):
+    real, imag = table[:KZ].T, table[KZ:].T
+    own = jnp.concatenate([real, imag], axis=1)
+    turned = jnp.concatenate([imag, -real], axis=1)
+    none = jnp.zeros_like(own)
+    halves = [[half, none] if field == 0 else [none, half] for half in (own, turned)]
+    return jnp.concatenate(halves[0] + halves[1], axis=1)
 
 
 def depth_forward(input_field, cotangent):
@@ -108,42 +117,44 @@
     planes = input_field.shape[1]
     rows = NY * C
     block = pl.BlockSpec((1, rows, NZ), lambda i: (i, 0, 0))
-    table = pl.BlockSpec((2 * KZ, NZ), lambda i: (0, 0))
+    table = pl.BlockSpec((NZ, 8 * KZ), lambda i: (0, 0))
     return pl.pallas_call(
         depth_kernel,
         grid=(planes,),
         in_specs=[block, block, table, table],
-        out_specs=pl.BlockSpec((2, 1, 2 * KZ, rows), lambda i: (0, i, 0, 0)),
-        out_shape=jax.ShapeDtypeStruct((2, planes, 2 * KZ, rows), bf16),
+        out_specs=pl.BlockSpec((1, rows, 8 * KZ), lambda i: (i, 0, 0)),
+        out_shape=jax.ShapeDtypeStruct((planes, rows, 8 * KZ), bf16),
         compiler_params=pltpu.CompilerParams(vmem_limit_bytes=40 * 2**20),
         name="depth_forward",
-    )(input_field.reshape(planes, rows, NZ), cotangent.reshape(planes, rows, NZ), plain, doubled)
+    )(
+        input_field.reshape(planes, rows, NZ),
+        cotangent.reshape(planes, rows, NZ),
+        lane_table(plain, 0),
+        lane_table(doubled, 1),
+    )
 
 
 def grid_kernel(rows_ref, output_table, grad_table, output_ref, grad_ref):
-    for k, (ref, table) in enumerate(((output_ref, output_table), (grad_ref, grad_table))):
+    for ref, table in ((output_ref, output_table), (grad_ref, grad_table)):
         ref[0] = (
-            lax.dot_general(
-                rows_ref[k, 0], table[...], (((0,), (0,)), ((), ())), preferred_element_type=f32
-            )
-            * norm_scale
+            jnp.dot(rows_ref[0], table[...], preferred_element_type=f32) * norm_scale
         ).astype(bf16)
 
 
 def depth_inverse(rows_in):
     plain, doubled = depth_tables()
-    planes, rows = rows_in.shape[1], NY * C
+    planes, rows = rows_in.shape[0], NY * C
     block = pl.BlockSpec((1, rows, NZ), lambda i: (i, 0, 0))
-    table = pl.BlockSpec((2 * KZ, NZ), lambda i: (0, 0))
+    table = pl.BlockSpec((8 * KZ, NZ), lambda i: (0, 0))
     outputs = pl.pallas_call(
         grid_kernel,
         grid=(planes,),
-        in_specs=[pl.BlockSpec((2, 1, 2 * KZ, rows), lambda i: (0, i, 0, 0)), table, table],
+        in_specs=[pl.BlockSpec((1, rows, 8 * KZ), lambda i: (i, 0, 0)), table, table],
         out_specs=[block, block],
         out_shape=[jax.ShapeDtypeStruct((planes, rows, NZ), bf16)] * 2,
         compiler_params=pltpu.CompilerParams(vmem_limit_bytes=40 * 2**20),
         name="depth_inverse",
-    )(rows_in, doubled, plain)
+    )(rows_in, lane_table(doubled, 0).T, lane_table(plain, 1).T)
     return [value.reshape(1, planes, NY, C, NZ) for value in outputs]
 
 
@@ -262,11 +273,13 @@
 
 def local(reps, input_field, cotangent, mode_weight, first_moment, second_moment):
     planes = input_field.shape[1]
-    rows = row_table()
-    depth = depth_forward(input_field, cotangent)
-    depth = depth.reshape(2, planes, 2, KZ, NY, C)
-    slabs = jnp.einsum("rpqy,fxpsyc->qsxfrc", rows, depth, preferred_element_type=f32)
-    slabs = slabs.astype(bf16).reshape(KY * KZ, planes, LANES)
+    cosine, sine = row_tables()
+    depth = depth_forward(input_field, cotangent).reshape(planes, NY, C, 8 * KZ)
+    slabs = jnp.einsum(
+        "qy,xycl->xqcl", cosine, depth[..., : 4 * KZ], preferred_element_type=f32
+    ) + jnp.einsum("qy,xycl->xqcl", sine, depth[..., 4 * KZ :], preferred_element_type=f32)
+    slabs = slabs.astype(bf16).reshape(planes, KY, C, 2, 2, KZ).transpose(1, 5, 0, 3, 4, 2)
+    slabs = slabs.reshape(KY * KZ, planes, LANES)
     columns = lax.all_to_all(slabs, "space", split_axis=0, concat_axis=1, tiled=True)
     modes = grid_modes(columns, reps)
     modes = lax.all_to_all(modes, "rep", split_axis=0, concat_axis=0, tiled=True)
@@ -276,9 +289,15 @@
     mixed = lax.all_to_all(mixed, "rep", split_axis=0, concat_axis=0, tiled=True)
     columns = mode_planes(mixed, reps)
     slabs = lax.all_to_all(columns, "space", split_axis=1, concat_axis=0, tiled=True)
-    slabs = slabs.reshape(KY, KZ, planes, 2, 2, C)
-    grid_rows = jnp.einsum("rpqy,qsxfrc->fxpsyc", rows, slabs, preferred_element_type=f32)
-    grid_rows = grid_rows.astype(bf16).reshape(2, planes, 2 * KZ, NY * C)
+    slabs = slabs.reshape(KY, KZ, planes, 2, 2, C).transpose(2, 0, 5, 3, 4, 1)
+    slabs = slabs.reshape(planes, KY, C, 4 * KZ)
+    grid_rows = jnp.concatenate(
+        [
+            jnp.einsum("qy,xqcl->xycl", table, slabs, preferred_element_type=f32).astype(bf16)
+            for table in (cosine, sine)
+        ],
+        axis=-1,
+    ).reshape(planes, NY * C, 8 * KZ)
     layer_output, input_gradient = depth_inverse(grid_rows)
     return (layer_output, input_gradient, new_weight, new_first, new_second)
 

time: 173 us -> 153 us (0.88)
  local copies, waits for them, and re-layouts: 83.3 us -> 54.5 us
  other arithmetic: 0 us -> 10.1 us
    reshape x4 -> x3, local copies, waits for them, and re-layouts: 40.8 us -> 4.82 us  [the longest x1 2.2 us: local(): slabs = slabs.reshape(planes, KY, C, 4 * KZ)]
    convert_element_type x2 -> x1, local copies, waits for them, and re-layouts: 16.4 us -> 1.99 us  [local(): slabs.astype(bf16).reshape(planes, KY, C, 2, 2, KZ)]
    concatenate x0 -> x1, local copies, waits for them, and re-layouts: none -> 12.6 us  [local(): jnp.concatenate([jnp.einsum('qy,xqcl->xycl', table, slabs, preferred_elem...]
    concatenate x0 -> x1, other arithmetic: none -> 10.1 us  [local(): jnp.concatenate([jnp.einsum('qy,xqcl->xycl', table, slabs, preferred_elem...]
    transpose x0 -> x2, local copies, waits for them, and re-layouts: none -> 6.29 us  [the longest x1 3.62 us: local(): slabs.astype(bf16).reshape(planes, KY, C, 2, 2, KZ)]
    slice x0 -> x1, local copies, waits for them, and re-layouts: none -> 3.79 us  [local(): depth[..., :4 * KZ]]
    unnamed x42 -> x34, local copies, waits for them, and re-layouts: 24.6 us -> 23.5 us
    dot_general x2 -> x4, matrix products: 11.1 us -> 11.4 us  [the longest x2 6.59 us: local(): jnp.einsum('qy,xqcl->xycl', table, slabs, preferred_element_type=f32)]
  transfers between devices with their start and end apart: 2 -> 2, of which waited for: 1 -> 1; matrix products, arithmetic and copies ran while one was open for 8% -> 11% of each run, Pallas kernels for 0% -> 0%
where the time goes in v1:
time: 153 us; the launch traced here: 151 us
  local copies, waits for them, and re-layouts  54.5 us (36%)
  Pallas kernels  30.9 us (20%)
  blocking collectives  29.3 us (19%)
  matrix products  11.4 us (7%)
  other arithmetic  10.1 us (7%)
  starting transfers between devices  7.65 us (5%)
  waiting for transfers between devices  6.7 us (4%)
    unnamed x34, local copies, waits for them, and re-layouts  23.5 us
    all_to_all x1, blocking collectives, local(): lax.all_to_all(slabs, 'space', split_axis=0, concat_axis=1, tiled=True)  22 us
    concatenate x1, local copies, waits for them, and re-layouts, local(): jnp.concatenate([jnp.einsum('qy,xqcl->xycl', table, slabs, preferred_elem...  12.6 us
    pallas_call x1, Pallas kernels, depth_forward(): pl.pallas_call(depth_kernel, grid=(planes,), in_specs=[block, block, tabl...  10.1 us
    concatenate x1, other arithmetic, local(): jnp.concatenate([jnp.einsum('qy,xqcl->xycl', table, slabs, preferred_elem...  10.1 us
    pallas_call x1, Pallas kernels, mix_and_update(): pl.pallas_call(mix_kernel, grid=(owned // step,), in_specs=[blocks, weigh...  8.66 us
    pallas_call x1, Pallas kernels, depth_inverse(): pl.pallas_call(grid_kernel, grid=(planes,), in_specs=[pl.BlockSpec((1, ro...  8.64 us
    all_to_all x1, blocking collectives, local(): lax.all_to_all(mixed, 'rep', split_axis=0, concat_axis=0, tiled=True)  7.35 us
  transfers between devices with their start and end apart: 2, of which 1 were waited for; matrix products, arithmetic and copies ran while one was open for 11% of the time, Pallas kernels for 0%

profile of v1, /device:TPU:0, one launch (start us, length us, event | category | flops | bytes accessed | tf_op | source)
XLA Modules:
  0.0 151.4 jit_solution(11144737522792076226)
XLA Ops:
  0.6 0.0 copy-start.6
  0.6 0.7 copy-done.6
  1.4 0.0 copy-start.7
  1.4 0.8 copy-done.7
  2.2 10.1 %depth_forward.1 = bf16[8,4096,128]{2,1,0:T(8,128)(2,1)S(1)} custom-call(bf16[8,4096,128]{2,1,0:T(8,128)(2,1)} %bitcast.44, bf16[8,4096,128]{2,1,0:T(8,128)(2,1)} %bitcast.45, bf16[128,128]{1,0:T(8,128)(2,1)S(1)} %copy-done.7, bf16[128,128]{1,0:T(8,128)(2,1)S(1)} %copy-done.6), custom_call_target="tpu_custom_call" | custom-call | tf_op jit(solution)/shard_map/depth_forward/pallas_call | solution.py:121
  12.3 0.0 copy-start.13
  12.3 3.8 %fusion.9 = (bf16[8,128,32,64]{3,2,1,0:T(8,128)(2,1)S(1)}, bf16[8,128,32,64]{3,2,1,0:T(8,128)(2,1)S(1)}) fusion(bf16[8,128,32,128]{3,2,1,0:T(8,128)(2,1)S(1)} %bitcast.41), kind=kLoop, calls=%fused_computation.11 | loop fusion | bytes 16777216 | tf_op jit(solution)/shard_map/slice | solution.py:279
  16.1 0.0 copy-start.12
  16.1 0.0 copy-done.13
  16.1 2.4 %fusion = f32[8,32,64,16]{2,3,1,0:T(8,128)S(1)} fusion(bf16[16,128,1,1]{1,0,3,2:T(8,128)(2,1)S(1)} %copy-done.13, bf16[8,128,32,64]{3,2,1,0:T(8,128)(2,1)S(1)} %get-tuple-element.38), kind=kOutput, calls=%fused_computation.1 | convolution fusion | flops 67108864 | bytes 5246976 | tf_op jit(solution)/shard_map/qy,xycl->xqcl/dot_general | solution.py:280
  18.5 0.0 copy-done.12
  18.5 2.5 %fusion.6 = bf16[8,16,32,64]{3,1,2,0:T(8,128)(2,1)S(1)} fusion(f32[8,32,64,16]{2,3,1,0:T(8,128)S(1)} %fusion, bf16[16,128,1,1]{1,0,3,2:T(8,128)(2,1)S(1)} %copy-done.12, bf16[8,128,32,64]{3,2,1,0:T(8,128)(2,1)S(1)} %get-tuple-element.37), kind=kOutput, calls=%fused_computation.8 | convolution fusion | flops 67633152 | bytes 5771264 | tf_op jit(solution)/shard_map/qy,xycl->xqcl/dot_general | solution.py:278
  21.0 0.0 copy-start.3
  21.0 0.0 copy-start.9
  21.0 2.0 %copy.64 = bf16[8,16,32,64]{2,3,1,0:T(8,128)(2,1)} copy(bf16[8,16,32,64]{3,1,2,0:T(8,128)(2,1)S(1)} %fusion.6) | data formatting | bytes 1048576 | tf_op jit(solution)/shard_map/convert_element_type | solution.py:281
  23.0 3.6 %copy.65 = bf16[16,16,8,2,2,32]{5,4,3,2,1,0:T(2,128)(2,1)S(1)} copy(bf16[16,16,8,2,2,32]{5,1,4,3,0,2:T(8,128)(2,1)} %bitcast.47) | data formatting | bytes 1048576 | tf_op jit(solution)/shard_map/transpose | solution.py:281
  26.6 0.0 copy-start.1
  26.6 1.8 %reshape.45 = bf16[256,8,128]{2,1,0:T(8,128)(2,1)} reshape(bf16[16,16,8,2,2,32]{5,4,3,2,1,0:T(2,128)(2,1)S(1)} %copy.65) | data formatting | bytes 1048576 | tf_op jit(solution)/shard_map/reshape | solution.py:282
  28.4 0.0 copy-start.11
  28.4 22.0 %all_to_all.43 = bf16[256,8,128]{2,1,0:T(8,128)(2,1)S(1)} all-to-all(bf16[256,8,128]{2,1,0:T(8,128)(2,1)} %reshape.45), channel_id=1, replica_groups=mesh['space'=16,'rep'=2] {'space'}, dimensions={0} | all-to-all | bytes 1048576 | tf_op jit(solution)/shard_map/all_to_all | solution.py:283
  50.3 0.1 copy.94
  50.5 0.0 copy-done.3
  50.5 0.0 copy-done.9
  50.5 1.2 grid_modes.1
  51.7 3.6 %all-to-all-start.1 = ((bf16[2,16,16,128]{3,2,1,0:T(8,128)(2,1)}), bf16[2,16,16,128]{3,2,1,0:T(8,128)(2,1)S(1)}, u32[]{:S(2)}, u32[]{:S(2)}) async-start(bf16[2,16,16,128]{3,2,1,0:T(8,128)(2,1)} %grid_modes.1), calls=%async_computation.1 | async-start | bytes 262144 | tf_op jit(solution)/shard_map/all_to_all | solution.py:285
  55.3 3.7 %copy.67.weight_ref = f32[16,12,2048]{2,1,0:T(8,128)} copy(f32[16,12,2048]{2,0,1:T(8,128)} %param.19) | data formatting | bytes 3145728 | tf_op args[2]
  58.9 0.0 copy-start.8
  58.9 3.7 %copy.68.first_ref = f32[16,12,2048]{2,1,0:T(8,128)} copy(f32[16,12,2048]{2,0,1:T(8,128)} %param.20) | data formatting | bytes 3145728 | tf_op args[3]
  62.6 0.0 copy-done.11
  62.6 2.3 %copy.69.second_ref = f32[16,12,2048]{2,1,0:T(8,128)} copy(f32[16,12,2048]{2,0,1:T(8,128)S(1)} %copy-done.11) | data formatting | bytes 3145728 | tf_op args[4]
  64.9 0.0 all-to-all-done.1.modes_ref
  64.9 0.0 copy-done.1
  64.9 0.0 copy-start.2
  64.9 1.2 copy-done.2
  66.1 8.7 %mix_and_update.1 = (bf16[2,16,16,128]{3,2,1,0:T(8,128)(2,1)S(1)}, f32[16,12,2048]{2,1,0:T(8,128)S(1)}, f32[16,12,2048]{2,1,0:T(8,128)}, f32[16,12,2048]{2,1,0:T(8,128)}) custom-call(bf16[2,16,16,128]{3,2,1,0:T(8,128)(2,1)S(1)} %all-to-all-done.1.modes_ref, f32[16,12,2048]{2,1,0:T(8,128)} %copy.67.weight_ref, f32[16,12,2048]{2,1,0:T(8,128)} %copy.68.first_ref, ...), custom_call_target="tpu_custom_call" | custom-call | tf_op jit(solution)/shard_map/mix_and_update/pallas_call | solution.py:255
  74.7 7.4 %all_to_all.44.modes_ref = bf16[2,16,16,128]{3,2,1,0:T(8,128)(2,1)S(1)} all-to-all(bf16[2,16,16,128]{3,2,1,0:T(8,128)(2,1)S(1)} %get-tuple-element.11), channel_id=1, replica_groups=mesh['space'=16,'rep'=2] {'rep'}, dimensions={0} | all-to-all | bytes 262144 | tf_op jit(solution)/shard_map/all_to_all | solution.py:289
  82.1 0.0 copy-done.8
  82.1 2.3 %mode_planes.1 = bf16[16,128,128]{2,1,0:T(8,128)(2,1)S(1)} custom-call(bf16[2,16,16,128]{3,2,1,0:T(8,128)(2,1)S(1)} %all_to_all.44.modes_ref, bf16[128,64]{1,0:T(8,128)(2,1)S(1)} %copy-done.8, bf16[128,128]{1,0:T(8,128)(2,1)S(1)} %copy-done.3), custom_call_target="tpu_custom_call" | custom-call | tf_op jit(solution)/shard_map/mode_planes/pallas_call | solution.py:194
  84.4 1.1 copy.70
  85.6 4.1 %all-to-all-start.3 = ((bf16[16,128,128]{2,0,1:T(8,128)(2,1)}), bf16[16,128,128]{2,0,1:T(8,128)(2,1)S(1)}, u32[]{:S(2)}, u32[]{:S(2)}) async-start(bf16[16,128,128]{2,0,1:T(8,128)(2,1)} %copy.70), calls=%async_computation.3 | async-start | bytes 1048576 | tf_op jit(solution)/shard_map/all_to_all | solution.py:291
  89.7 0.0 copy-start.10
  89.7 2.1 %copy.76 = f32[16,12,2048]{2,0,1:T(8,128)} copy(f32[16,12,2048]{2,1,0:T(8,128)S(1)} %get-tuple-element.34) | data formatting | bytes 3145728
  91.7 3.6 %copy.77 = f32[16,12,2048]{2,0,1:T(8,128)} copy(f32[16,12,2048]{2,1,0:T(8,128)} %get-tuple-element.35) | data formatting | bytes 3145728
  95.4 0.0 copy-done.10
  95.4 2.1 %copy.78 = f32[16,12,2048]{2,0,1:T(8,128)} copy(f32[16,12,2048]{2,1,0:T(8,128)S(1)} %copy-done.10) | data formatting | bytes 3145728
  97.4 6.7 %all-to-all-done.3 = bf16[16,128,128]{2,0,1:T(8,128)(2,1)S(1)} async-done(((bf16[16,128,128]{2,0,1:T(8,128)(2,1)}), bf16[16,128,128]{2,0,1:T(8,128)(2,1)S(1)}, u32[]{:S(2)}, u32[]{:S(2)}) %all-to-all-start.3) | async-done | bytes 524320 | tf_op jit(solution)/shard_map/all_to_all | solution.py:291
  104.1 0.1 copy.93
  104.3 0.9 reshape.46
  105.1 2.7 %copy.72 = bf16[8,16,32,2,2,16]{2,5,4,3,1,0:T(8,128)(2,1)} copy(bf16[8,16,32,2,2,16]{2,4,3,0,5,1:T(2,128)(2,1)S(1)} %bitcast.46) | data formatting | bytes 1048576 | tf_op jit(solution)/shard_map/transpose | solution.py:292
  107.8 2.2 %copy.73 = bf16[8,16,32,64]{3,1,2,0:T(8,128)(2,1)S(1)} copy(bf16[8,16,32,64]{2,3,1,0:T(8,128)(2,1)} %bitcast.48) | data formatting | bytes 1048576 | tf_op jit(solution)/shard_map/reshape | solution.py:293
  110.0 3.3 %convert_bitcast_fusion = bf16[8,128,32,64]{1,3,2,0:T(8,128)(2,1)} fusion(bf16[8,16,32,64]{3,1,2,0:T(8,128)(2,1)S(1)} %copy.73, bf16[16,128,1,1]{1,0,3,2:T(8,128)(2,1)S(1)} %copy-done.13), kind=kOutput, calls=%fused_computation.5 | convolution fusion | flops 69206016 | bytes 4722688 | tf_op jit(solution)/shard_map/qy,xqcl->xycl/dot_general | solution.py:296
  113.3 3.3 %convert_bitcast_fusion.1 = bf16[8,128,32,64]{1,3,2,0:T(8,128)(2,1)} fusion(bf16[8,16,32,64]{3,1,2,0:T(8,128)(2,1)S(1)} %copy.73, bf16[16,128,1,1]{1,0,3,2:T(8,128)(2,1)S(1)} %copy-done.12), kind=kOutput, calls=%fused_computation.6 | convolution fusion | flops 69206016 | bytes 4722688 | tf_op jit(solution)/shard_map/qy,xqcl->xycl/dot_general | solution.py:296
  116.6 10.1 %pad_maximum_fusion = bf16[8,128,32,128]{1,3,2,0:T(8,128)(2,1)} fusion(bf16[8,128,32,64]{1,3,2,0:T(8,128)(2,1)} %convert_bitcast_fusion, bf16[8,128,32,64]{1,3,2,0:T(8,128)(2,1)} %convert_bitcast_fusion.1), kind=kLoop, calls=%fused_computation | loop fusion | flops 16777216 | bytes 16777216 | tf_op jit(solution)/shard_map/concatenate | solution.py:294
  126.7 0.0 copy-start.4
  126.7 0.0 copy-start.5
  126.7 12.6 %copy.75 = bf16[8,128,32,128]{3,2,1,0:T(8,128)(2,1)} copy(bf16[8,128,32,128]{1,3,2,0:T(8,128)(2,1)} %pad_maximum_fusion) | data formatting | bytes 16777216 | tf_op jit(solution)/shard_map/concatenate | solution.py:294
  139.4 0.0 copy-done.4
  139.4 0.0 copy-done.5
  139.4 0.0 copy-start
  139.4 3.4 %copy-done = bf16[8,128,32,128]{3,2,1,0:T(8,128)(2,1)S(1)} copy-done((bf16[8,128,32,128]{3,2,1,0:T(8,128)(2,1)S(1)}, bf16[8,128,32,128]{3,2,1,0:T(8,128)(2,1)}, u32[]{:S(2)}) %copy-start) | copy-done | bytes 8388632
  142.8 8.6 %depth_inverse.1 = (bf16[8,4096,128]{2,1,0:T(8,128)(2,1)}, bf16[8,4096,128]{2,1,0:T(8,128)(2,1)}) custom-call(bf16[8,4096,128]{2,1,0:T(8,128)(2,1)S(1)} %bitcast.42, bf16[128,128]{1,0:T(8,128)(2,1)S(1)} %copy-done.5, bf16[128,128]{1,0:T(8,128)(2,1)S(1)} %copy-done.4), custom_call_target="tpu_custom_call" | custom-call | tf_op jit(solution)/shard_map/depth_inverse/pallas_call | solution.py:149
Async XLA Ops:
  0.6 0.8 copy-start.6
  1.4 0.8 copy-start.7
  12.3 3.8 %copy-start.13 = (bf16[16,128,1,1]{1,0,3,2:T(8,128)(2,1)S(1)}, bf16[16,128,1,1]{1,0,3,2:T(8,128)(2,1)}, u32[]{:S(2)}) copy-start(bf16[16,128,1,1]{1,0,3,2:T(8,128)(2,1)} %constant.48) | copy-start | bytes 12292
  16.1 2.4 %copy-start.12 = (bf16[16,128,1,1]{1,0,3,2:T(8,128)(2,1)S(1)}, bf16[16,128,1,1]{1,0,3,2:T(8,128)(2,1)}, u32[]{:S(2)}) copy-start(bf16[16,128,1,1]{1,0,3,2:T(8,128)(2,1)} %constant.47) | copy-start | bytes 12292
  21.0 29.5 %copy-start.3 = (bf16[128,128]{1,0:T(8,128)(2,1)S(1)}, bf16[128,128]{1,0:T(8,128)(2,1)}, u32[]{:S(2)}) copy-start(bf16[128,128]{1,0:T(8,128)(2,1)} %constant.25.clone.turn_ref) | copy-start | bytes 98308
  21.0 29.5 %copy-start.9 = (bf16[32,256]{1,0:T(8,128)(2,1)S(1)}, bf16[32,256]{1,0:T(8,128)(2,1)}, u32[]{:S(2)}) copy-start(bf16[32,256]{1,0:T(8,128)(2,1)} %constant.24.clone.table_ref) | copy-start | bytes 49156
  26.6 38.3 %copy-start.1 = (bf16[4,1024,128]{2,1,0:T(8,128)(2,1)S(1)}, bf16[4,1024,128]{2,1,0:T(8,128)(2,1)}, u32[]{:S(2)}) copy-start(bf16[4,1024,128]{2,1,0:T(8,128)(2,1)} %constant.27.clone.gather_ref) | copy-start | bytes 3145732
  28.4 34.2 %copy-start.11 = (f32[16,12,2048]{2,0,1:T(8,128)S(1)}, f32[16,12,2048]{2,0,1:T(8,128)}, u32[]{:S(2)}) copy-start(f32[16,12,2048]{2,0,1:T(8,128)} %param.21) | copy-start | bytes 4718596
  51.7 13.2 %all-to-all-start.1 = ((bf16[2,16,16,128]{3,2,1,0:T(8,128)(2,1)}), bf16[2,16,16,128]{3,2,1,0:T(8,128)(2,1)S(1)}, u32[]{:S(2)}, u32[]{:S(2)}) async-start(bf16[2,16,16,128]{3,2,1,0:T(8,128)(2,1)} %grid_modes.1), calls=%async_computation.1 | async-start | bytes 262144 | tf_op jit(solution)/shard_map/all_to_all | solution.py:285
  58.9 23.2 %copy-start.8 = (bf16[128,64]{1,0:T(8,128)(2,1)S(1)}, bf16[128,64]{1,0:T(8,128)(2,1)}, u32[]{:S(2)}) copy-start(bf16[128,64]{1,0:T(8,128)(2,1)} %constant.28.clone.table_ref) | copy-start | bytes 49156
  64.9 1.2 copy-start.2
  85.6 18.6 %all-to-all-start.3 = ((bf16[16,128,128]{2,0,1:T(8,128)(2,1)}), bf16[16,128,128]{2,0,1:T(8,128)(2,1)S(1)}, u32[]{:S(2)}, u32[]{:S(2)}) async-start(bf16[16,128,128]{2,0,1:T(8,128)(2,1)} %copy.70), calls=%async_computation.3 | async-start | bytes 1048576 | tf_op jit(solution)/shard_map/all_to_all | solution.py:291
  89.7 5.7 %copy-start.10 = (f32[16,12,2048]{2,1,0:T(8,128)S(1)}, f32[16,12,2048]{2,1,0:T(8,128)}, u32[]{:S(2)}) copy-start(f32[16,12,2048]{2,1,0:T(8,128)} %get-tuple-element.36) | copy-start | bytes 4718596
  126.7 12.7 %copy-start.4 = (bf16[128,128]{1,0:T(8,128)(2,1)S(1)}, bf16[128,128]{1,0:T(8,128)(2,1)}, u32[]{:S(2)}) copy-start(bf16[128,128]{1,0:T(8,128)(2,1)} %constant.46.grad_table) | copy-start | bytes 98308
  126.7 12.7 %copy-start.5 = (bf16[128,128]{1,0:T(8,128)(2,1)S(1)}, bf16[128,128]{1,0:T(8,128)(2,1)}, u32[]{:S(2)}) copy-start(bf16[128,128]{1,0:T(8,128)(2,1)} %constant.44.output_table) | copy-start | bytes 98308
  139.4 3.4 %copy-start = (bf16[8,128,32,128]{3,2,1,0:T(8,128)(2,1)S(1)}, bf16[8,128,32,128]{3,2,1,0:T(8,128)(2,1)}, u32[]{:S(2)}) copy-start(bf16[8,128,32,128]{3,2,1,0:T(8,128)(2,1)} %copy.75) | copy-start | bytes 25165828

commit v2 on v1

--- a/solution.py
+++ b/solution.py
@@ -145,16 +145,16 @@
     plain, doubled = depth_tables()
     planes, rows = rows_in.shape[0], NY * C
     block = pl.BlockSpec((1, rows, NZ), lambda i: (i, 0, 0))
-    table = pl.BlockSpec((8 * KZ, NZ), lambda i: (0, 0))
+    table = pl.BlockSpec((4 * KZ, NZ), lambda i: (0, 0))
     outputs = pl.pallas_call(
         grid_kernel,
         grid=(planes,),
-        in_specs=[pl.BlockSpec((1, rows, 8 * KZ), lambda i: (i, 0, 0)), table, table],
+        in_specs=[pl.BlockSpec((1, rows, 4 * KZ), lambda i: (i, 0, 0)), table, table],
         out_specs=[block, block],
         out_shape=[jax.ShapeDtypeStruct((planes, rows, NZ), bf16)] * 2,
         compiler_params=pltpu.CompilerParams(vmem_limit_bytes=40 * 2**20),
         name="depth_inverse",
-    )(rows_in, lane_table(doubled, 0).T, lane_table(plain, 1).T)
+    )(rows_in, lane_table(doubled, 0)[:, : 4 * KZ].T, lane_table(plain, 1)[:, : 4 * KZ].T)
     return [value.reshape(1, planes, NY, C, NZ) for value in outputs]
 
 
@@ -290,14 +290,11 @@
     columns = mode_planes(mixed, reps)
     slabs = lax.all_to_all(columns, "space", split_axis=1, concat_axis=0, tiled=True)
     slabs = slabs.reshape(KY, KZ, planes, 2, 2, C).transpose(2, 0, 5, 3, 4, 1)
-    slabs = slabs.reshape(planes, KY, C, 4 * KZ)
-    grid_rows = jnp.concatenate(
-        [
-            jnp.einsum("qy,xqcl->xycl", table, slabs, preferred_element_type=f32).astype(bf16)
-            for table in (cosine, sine)
-        ],
-        axis=-1,
-    ).reshape(planes, NY * C, 8 * KZ)
+    turned = jnp.stack([-slabs[:, :, :, :, 1], slabs[:, :, :, :, 0]], axis=4)
+    slabs = jnp.concatenate([slabs, turned], axis=1).reshape(planes, 2 * KY, C, 4 * KZ)
+    table = jnp.concatenate([cosine, sine], axis=0)
+    grid_rows = jnp.einsum("qy,xqcl->xycl", table, slabs, preferred_element_type=f32)
+    grid_rows = grid_rows.astype(bf16).reshape(planes, NY * C, 4 * KZ)
     layer_output, input_gradient = depth_inverse(grid_rows)
     return (layer_output, input_gradient, new_weight, new_first, new_second)
 

time: 153 us -> 156 us (1.020)
  local copies, waits for them, and re-layouts: 54.5 us -> 58.7 us
  matrix products: 11.4 us -> 8.19 us
  other arithmetic: 10.1 us -> 13.1 us
    convert_element_type x0 -> x1, local copies, waits for them, and re-layouts: none -> 12.8 us  [local(): grid_rows = grid_rows.astype(bf16).reshape(planes, NY * C, 4 * KZ)]
    concatenate x1, local copies, waits for them, and re-layouts: 12.6 us -> 4.71 us  [local(): jnp.concatenate([slabs, turned], axis=1).reshape(planes, 2 * KY, C, 4 * KZ)]
    neg x0 -> x1, other arithmetic: none -> 4.67 us  [local(): turned = jnp.stack([-slabs[:, :, :, :, 1], slabs[:, :, :, :, 0]], axis=4)]
    dot_general x2 -> x1, matrix products: 6.59 us -> 3.34 us  [local(): jnp.einsum('qy,xqcl->xycl', table, slabs, preferred_element_type=f32)]
    reshape x1, local copies, waits for them, and re-layouts: 2.2 us -> 4.9 us  [local(): jnp.concatenate([slabs, turned], axis=1).reshape(planes, 2 * KY, C, 4 * KZ)]
    transpose x1 -> x0, local copies, waits for them, and re-layouts: 2.67 us -> none  [local(): slabs = slabs.reshape(KY, KZ, planes, 2, 2, C).transpose(2, 0, 5, 3, 4, 1)]
    concatenate x1, other arithmetic: 10.1 us -> 8.39 us  [local(): jnp.concatenate([slabs, turned], axis=1).reshape(planes, 2 * KY, C, 4 * KZ)]
    unnamed x34 -> x36, local copies, waits for them, and re-layouts: 23.5 us -> 23.5 us
where the time goes in v2:
time: 156 us; the launch traced here: 155 us
  local copies, waits for them, and re-layouts  58.7 us (38%)
  Pallas kernels  30.9 us (20%)
  blocking collectives  29 us (19%)
  other arithmetic  13.1 us (8%)
  matrix products  8.19 us (5%)
  starting transfers between devices  7.65 us (5%)
  waiting for transfers between devices  6.7 us (4%)
    unnamed x36, local copies, waits for them, and re-layouts  23.5 us
    all_to_all x1, blocking collectives, local(): lax.all_to_all(slabs, 'space', split_axis=0, concat_axis=1, tiled=True)  21.6 us
    convert_element_type x1, local copies, waits for them, and re-layouts, local(): grid_rows = grid_rows.astype(bf16).reshape(planes, NY * C, 4 * KZ)  12.8 us
    pallas_call x1, Pallas kernels, depth_forward(): pl.pallas_call(depth_kernel, grid=(planes,), in_specs=[block, block, tabl...  10.1 us
    pallas_call x1, Pallas kernels, mix_and_update(): pl.pallas_call(mix_kernel, grid=(owned // step,), in_specs=[blocks, weigh...  8.66 us
    pallas_call x1, Pallas kernels, depth_inverse(): pl.pallas_call(grid_kernel, grid=(planes,), in_specs=[pl.BlockSpec((1, ro...  8.59 us
    concatenate x1, other arithmetic, local(): jnp.concatenate([slabs, turned], axis=1).reshape(planes, 2 * KY, C, 4 * KZ)  8.39 us
    all_to_all x1, blocking collectives, local(): lax.all_to_all(mixed, 'rep', split_axis=0, concat_axis=0, tiled=True)  7.36 us
  transfers between devices with their start and end apart: 2, of which 1 were waited for; matrix products, arithmetic and copies ran while one was open for 11% of the time, Pallas kernels for 0%

profile of v2, /device:TPU:0, one launch (start us, length us, event | category | flops | bytes accessed | tf_op | source)
XLA Modules:
  0.0 155.0 jit_solution(17876733318061117890)
XLA Ops:
  0.6 0.0 copy-start.4
  0.6 0.7 copy-done.4
  1.4 0.0 copy-start.5
  1.4 0.8 copy-done.5
  2.2 10.1 %depth_forward.1 = bf16[8,4096,128]{2,1,0:T(8,128)(2,1)S(1)} custom-call(bf16[8,4096,128]{2,1,0:T(8,128)(2,1)} %bitcast.46, bf16[8,4096,128]{2,1,0:T(8,128)(2,1)} %bitcast.47, bf16[128,128]{1,0:T(8,128)(2,1)S(1)} %copy-done.5, bf16[128,128]{1,0:T(8,128)(2,1)S(1)} %copy-done.4), custom_call_target="tpu_custom_call" | custom-call | tf_op jit(solution)/shard_map/depth_forward/pallas_call | solution.py:121
  12.3 0.0 copy-start.14
  12.3 3.8 %fusion.9 = (bf16[8,128,32,64]{3,2,1,0:T(8,128)(2,1)S(1)}, bf16[8,128,32,64]{3,2,1,0:T(8,128)(2,1)S(1)}) fusion(bf16[8,128,32,128]{3,2,1,0:T(8,128)(2,1)S(1)} %bitcast.40), kind=kLoop, calls=%fused_computation.11 | loop fusion | bytes 16777216 | tf_op jit(solution)/shard_map/slice | solution.py:279
  16.1 0.0 copy-done.14
  16.1 0.0 copy-start.13
  16.1 2.4 %fusion = f32[8,32,64,16]{2,3,1,0:T(8,128)S(1)} fusion(bf16[16,128,1,1]{1,0,3,2:T(8,128)(2,1)S(1)} %copy-done.14, bf16[8,128,32,64]{3,2,1,0:T(8,128)(2,1)S(1)} %get-tuple-element.38), kind=kOutput, calls=%fused_computation | convolution fusion | flops 67108864 | bytes 5246976 | tf_op jit(solution)/shard_map/qy,xycl->xqcl/dot_general | solution.py:280
  18.5 0.0 copy-done.13
  18.5 2.5 %fusion.6 = bf16[8,16,32,64]{3,1,2,0:T(8,128)(2,1)S(1)} fusion(f32[8,32,64,16]{2,3,1,0:T(8,128)S(1)} %fusion, bf16[16,128,1,1]{1,0,3,2:T(8,128)(2,1)S(1)} %copy-done.13, bf16[8,128,32,64]{3,2,1,0:T(8,128)(2,1)S(1)} %get-tuple-element.37), kind=kOutput, calls=%fused_computation.8 | convolution fusion | flops 67633152 | bytes 5771264 | tf_op jit(solution)/shard_map/qy,xycl->xqcl/dot_general | solution.py:278
  21.0 2.0 %copy.62 = bf16[8,16,32,64]{2,3,1,0:T(8,128)(2,1)} copy(bf16[8,16,32,64]{3,1,2,0:T(8,128)(2,1)S(1)} %fusion.6) | data formatting | bytes 1048576 | tf_op jit(solution)/shard_map/convert_element_type | solution.py:281
  23.0 0.0 copy-start.3
  23.0 0.0 copy-start.9
  23.0 3.6 %copy.63 = bf16[16,16,8,2,2,32]{5,4,3,2,1,0:T(2,128)(2,1)S(1)} copy(bf16[16,16,8,2,2,32]{5,1,4,3,0,2:T(8,128)(2,1)} %bitcast.48) | data formatting | bytes 1048576 | tf_op jit(solution)/shard_map/transpose | solution.py:281
  26.6 1.1 reshape.45
  27.7 21.6 %all_to_all.43 = bf16[256,8,128]{2,1,0:T(8,128)(2,1)S(1)} all-to-all(bf16[256,8,128]{2,1,0:T(8,128)(2,1)S(1)} %reshape.45), channel_id=1, replica_groups=mesh['space'=16,'rep'=2] {'space'}, dimensions={0} | all-to-all | bytes 1048576 | tf_op jit(solution)/shard_map/all_to_all | solution.py:283
  49.3 0.1 copy.92
  49.4 0.0 copy-start.11
  49.4 0.0 copy-done.3
  49.4 0.0 copy-done.9
  49.5 1.2 grid_modes.1
  50.6 3.6 %all-to-all-start.1 = ((bf16[2,16,16,128]{3,2,1,0:T(8,128)(2,1)}), bf16[2,16,16,128]{3,2,1,0:T(8,128)(2,1)S(1)}, u32[]{:S(2)}, u32[]{:S(2)}) async-start(bf16[2,16,16,128]{3,2,1,0:T(8,128)(2,1)} %grid_modes.1), calls=%async_computation.1 | async-start | bytes 262144 | tf_op jit(solution)/shard_map/all_to_all | solution.py:285
  54.2 3.7 %copy.65.weight_ref = f32[16,12,2048]{2,1,0:T(8,128)} copy(f32[16,12,2048]{2,0,1:T(8,128)} %param.19) | data formatting | bytes 3145728 | tf_op args[2]
  57.9 0.0 copy-done.11
  57.9 0.0 copy-start.1
  57.9 2.2 %copy.66.first_ref = f32[16,12,2048]{2,1,0:T(8,128)} copy(f32[16,12,2048]{2,0,1:T(8,128)S(1)} %copy-done.11) | data formatting | bytes 3145728 | tf_op args[3]
  60.1 3.7 %copy.67.second_ref = f32[16,12,2048]{2,1,0:T(8,128)} copy(f32[16,12,2048]{2,0,1:T(8,128)} %param.21) | data formatting | bytes 3145728 | tf_op args[4]
  63.8 0.0 all-to-all-done.1.modes_ref
  63.8 0.0 copy-done.1
  63.8 0.0 copy-start.2
  63.8 1.2 copy-done.2
  65.0 0.0 copy-start.6
  65.0 8.7 %mix_and_update.1 = (bf16[2,16,16,128]{3,2,1,0:T(8,128)(2,1)S(1)}, f32[16,12,2048]{2,1,0:T(8,128)S(1)}, f32[16,12,2048]{2,1,0:T(8,128)}, f32[16,12,2048]{2,1,0:T(8,128)}) custom-call(bf16[2,16,16,128]{3,2,1,0:T(8,128)(2,1)S(1)} %all-to-all-done.1.modes_ref, f32[16,12,2048]{2,1,0:T(8,128)} %copy.65.weight_ref, f32[16,12,2048]{2,1,0:T(8,128)} %copy.66.first_ref, ...), custom_call_target="tpu_custom_call" | custom-call | tf_op jit(solution)/shard_map/mix_and_update/pallas_call | solution.py:255
  73.7 7.4 %all_to_all.44.modes_ref = bf16[2,16,16,128]{3,2,1,0:T(8,128)(2,1)S(1)} all-to-all(bf16[2,16,16,128]{3,2,1,0:T(8,128)(2,1)S(1)} %get-tuple-element.11), channel_id=1, replica_groups=mesh['space'=16,'rep'=2] {'rep'}, dimensions={0} | all-to-all | bytes 262144 | tf_op jit(solution)/shard_map/all_to_all | solution.py:289
  81.1 0.0 copy-done.6
  81.1 2.3 %mode_planes.1 = bf16[16,128,128]{2,1,0:T(8,128)(2,1)S(1)} custom-call(bf16[2,16,16,128]{3,2,1,0:T(8,128)(2,1)S(1)} %all_to_all.44.modes_ref, bf16[128,64]{1,0:T(8,128)(2,1)S(1)} %copy-done.6, bf16[128,128]{1,0:T(8,128)(2,1)S(1)} %copy-done.3), custom_call_target="tpu_custom_call" | custom-call | tf_op jit(solution)/shard_map/mode_planes/pallas_call | solution.py:194
  83.4 1.1 copy.68
  84.5 4.1 %all-to-all-start.3 = ((bf16[16,128,128]{2,0,1:T(8,128)(2,1)}), bf16[16,128,128]{2,0,1:T(8,128)(2,1)S(1)}, u32[]{:S(2)}, u32[]{:S(2)}) async-start(bf16[16,128,128]{2,0,1:T(8,128)(2,1)} %copy.68), calls=%async_computation.3 | async-start | bytes 1048576 | tf_op jit(solution)/shard_map/all_to_all | solution.py:291
  88.6 0.0 copy-start.10
  88.6 2.1 %copy.73 = f32[16,12,2048]{2,0,1:T(8,128)} copy(f32[16,12,2048]{2,1,0:T(8,128)S(1)} %get-tuple-element.34) | data formatting | bytes 3145728
  90.7 3.6 %copy.74 = f32[16,12,2048]{2,0,1:T(8,128)} copy(f32[16,12,2048]{2,1,0:T(8,128)} %get-tuple-element.35) | data formatting | bytes 3145728
  94.3 0.0 copy-done.10
  94.3 2.1 %copy.75 = f32[16,12,2048]{2,0,1:T(8,128)} copy(f32[16,12,2048]{2,1,0:T(8,128)S(1)} %copy-done.10) | data formatting | bytes 3145728
  96.4 6.7 %all-to-all-done.3 = bf16[16,128,128]{2,0,1:T(8,128)(2,1)S(1)} async-done(((bf16[16,128,128]{2,0,1:T(8,128)(2,1)}), bf16[16,128,128]{2,0,1:T(8,128)(2,1)S(1)}, u32[]{:S(2)}, u32[]{:S(2)}) %all-to-all-start.3) | async-done | bytes 524320 | tf_op jit(solution)/shard_map/all_to_all | solution.py:291
  103.1 0.1 copy.91
  103.2 0.9 reshape.46
  104.1 4.7 %slice_negate_fusion = (bf16[8,16,32,2,1,16]{2,4,3,0,5,1:T(2,128)(2,1)S(1)}, bf16[8,16,32,2,1,16]{2,4,3,0,5,1:T(2,128)(2,1)S(1)}) fusion(bf16[8,16,32,2,2,16]{2,4,3,0,5,1:T(2,128)(2,1)S(1)} %bitcast.43), kind=kLoop, calls=%fused_computation.6 | loop fusion | flops 131072 | bytes 1048576 | tf_op jit(solution)/shard_map/neg | solution.py:293
  108.8 8.4 %maximum_maximum_fusion = bf16[8,32,32,2,2,16]{2,4,3,0,5,1:T(2,128)(2,1)S(1)} fusion(bf16[8,16,32,2,1,16]{2,4,3,0,5,1:T(2,128)(2,1)S(1)} %get-tuple-element.40, bf16[8,16,32,2,1,16]{2,4,3,0,5,1:T(2,128)(2,1)S(1)} %get-tuple-element.39, bf16[8,16,32,2,2,16]{2,4,3,0,5,1:T(2,128)(2,1)S(1)} %bitcast.44), kind=kLoop, calls=%fused_computation.4 | loop fusion | flops 3145728 | bytes 2097152 | tf_op jit(solution)/shard_map/concatenate | solution.py:294
  117.2 4.7 %copy.70 = bf16[8,32,32,2,2,16]{2,5,4,3,1,0:T(8,128)(2,1)} copy(bf16[8,32,32,2,2,16]{2,4,3,0,5,1:T(2,128)(2,1)S(1)} %maximum_maximum_fusion) | data formatting | bytes 2097152 | tf_op jit(solution)/shard_map/concatenate | solution.py:294
  121.9 0.0 copy-start.12
  121.9 4.9 %copy.71 = bf16[8,32,32,64]{3,1,2,0:T(8,128)(2,1)S(1)} copy(bf16[8,32,32,64]{2,3,1,0:T(8,128)(2,1)} %bitcast.45) | data formatting | bytes 2097152 | tf_op jit(solution)/shard_map/reshape | solution.py:294
  126.8 0.0 copy-done.12
  126.8 3.3 %convert_bitcast_fusion = bf16[8,128,32,64]{1,3,2,0:T(8,128)(2,1)} fusion(bf16[8,32,32,64]{3,1,2,0:T(8,128)(2,1)S(1)} %copy.71, bf16[32,128,1,1]{1,0,3,2:T(8,128)(2,1)S(1)} %copy-done.12), kind=kOutput, calls=%fused_computation.5 | convolution fusion | flops 136314880 | bytes 5251072 | tf_op jit(solution)/shard_map/qy,xqcl->xycl/dot_general | solution.py:296
  130.1 0.0 copy-start.7
  130.1 0.0 copy-start.8
  130.1 12.8 %copy.72 = bf16[8,128,32,64]{3,2,1,0:T(8,128)(2,1)} copy(bf16[8,128,32,64]{1,3,2,0:T(8,128)(2,1)} %convert_bitcast_fusion) | data formatting | bytes 8388608 | tf_op jit(solution)/shard_map/convert_element_type | solution.py:297
  143.0 0.0 copy-done.7
  143.0 0.0 copy-done.8
  143.0 0.0 copy-start
  143.0 3.4 %copy-done = bf16[8,128,32,64]{3,2,1,0:T(8,128)(2,1)S(1)} copy-done((bf16[8,128,32,64]{3,2,1,0:T(8,128)(2,1)S(1)}, bf16[8,128,32,64]{3,2,1,0:T(8,128)(2,1)}, u32[]{:S(2)}) %copy-start) | copy-done | bytes 4194328
  146.4 8.6 %depth_inverse.1 = (bf16[8,4096,128]{2,1,0:T(8,128)(2,1)}, bf16[8,4096,128]{2,1,0:T(8,128)(2,1)}) custom-call(bf16[8,4096,64]{2,1,0:T(8,128)(2,1)S(1)} %bitcast.41, bf16[64,128]{1,0:T(8,128)(2,1)S(1)} %copy-done.8, bf16[64,128]{1,0:T(8,128)(2,1)S(1)} %copy-done.7), custom_call_target="tpu_custom_call" | custom-call | tf_op jit(solution)/shard_map/depth_inverse/pallas_call | solution.py:149
Async XLA Ops:
  0.6 0.8 copy-start.4
  1.4 0.8 copy-start.5
  12.3 3.8 %copy-start.14 = (bf16[16,128,1,1]{1,0,3,2:T(8,128)(2,1)S(1)}, bf16[16,128,1,1]{1,0,3,2:T(8,128)(2,1)}, u32[]{:S(2)}) copy-start(bf16[16,128,1,1]{1,0,3,2:T(8,128)(2,1)} %constant.49) | copy-start | bytes 12292
  16.1 2.4 %copy-start.13 = (bf16[16,128,1,1]{1,0,3,2:T(8,128)(2,1)S(1)}, bf16[16,128,1,1]{1,0,3,2:T(8,128)(2,1)}, u32[]{:S(2)}) copy-start(bf16[16,128,1,1]{1,0,3,2:T(8,128)(2,1)} %constant.48) | copy-start | bytes 12292
  23.0 26.5 %copy-start.3 = (bf16[128,128]{1,0:T(8,128)(2,1)S(1)}, bf16[128,128]{1,0:T(8,128)(2,1)}, u32[]{:S(2)}) copy-start(bf16[128,128]{1,0:T(8,128)(2,1)} %constant.25.clone.turn_ref) | copy-start | bytes 98308
  23.0 26.5 %copy-start.9 = (bf16[32,256]{1,0:T(8,128)(2,1)S(1)}, bf16[32,256]{1,0:T(8,128)(2,1)}, u32[]{:S(2)}) copy-start(bf16[32,256]{1,0:T(8,128)(2,1)} %constant.24.clone.table_ref) | copy-start | bytes 49156
  49.4 8.5 %copy-start.11 = (f32[16,12,2048]{2,0,1:T(8,128)S(1)}, f32[16,12,2048]{2,0,1:T(8,128)}, u32[]{:S(2)}) copy-start(f32[16,12,2048]{2,0,1:T(8,128)} %param.20) | copy-start | bytes 4718596
  50.6 13.2 %all-to-all-start.1 = ((bf16[2,16,16,128]{3,2,1,0:T(8,128)(2,1)}), bf16[2,16,16,128]{3,2,1,0:T(8,128)(2,1)S(1)}, u32[]{:S(2)}, u32[]{:S(2)}) async-start(bf16[2,16,16,128]{3,2,1,0:T(8,128)(2,1)} %grid_modes.1), calls=%async_computation.1 | async-start | bytes 262144 | tf_op jit(solution)/shard_map/all_to_all | solution.py:285
  57.9 5.9 %copy-start.1 = (bf16[4,1024,128]{2,1,0:T(8,128)(2,1)S(1)}, bf16[4,1024,128]{2,1,0:T(8,128)(2,1)}, u32[]{:S(2)}) copy-start(bf16[4,1024,128]{2,1,0:T(8,128)(2,1)} %constant.27.clone.gather_ref) | copy-start | bytes 3145732
  63.8 1.2 copy-start.2
  65.0 16.0 %copy-start.6 = (bf16[128,64]{1,0:T(8,128)(2,1)S(1)}, bf16[128,64]{1,0:T(8,128)(2,1)}, u32[]{:S(2)}) copy-start(bf16[128,64]{1,0:T(8,128)(2,1)} %constant.28.clone.table_ref) | copy-start | bytes 49156
  84.5 18.6 %all-to-all-start.3 = ((bf16[16,128,128]{2,0,1:T(8,128)(2,1)}), bf16[16,128,128]{2,0,1:T(8,128)(2,1)S(1)}, u32[]{:S(2)}, u32[]{:S(2)}) async-start(bf16[16,128,128]{2,0,1:T(8,128)(2,1)} %copy.68), calls=%async_computation.3 | async-start | bytes 1048576 | tf_op jit(solution)/shard_map/all_to_all | solution.py:291
  88.6 5.7 %copy-start.10 = (f32[16,12,2048]{2,1,0:T(8,128)S(1)}, f32[16,12,2048]{2,1,0:T(8,128)}, u32[]{:S(2)}) copy-start(f32[16,12,2048]{2,1,0:T(8,128)} %get-tuple-element.36) | copy-start | bytes 4718596
  121.9 4.9 %copy-start.12 = (bf16[32,128,1,1]{1,0,3,2:T(8,128)(2,1)S(1)}, bf16[32,128,1,1]{1,0,3,2:T(8,128)(2,1)}, u32[]{:S(2)}) copy-start(bf16[32,128,1,1]{1,0,3,2:T(8,128)(2,1)} %constant.50) | copy-start | bytes 24580
  130.1 12.8 %copy-start.7 = (bf16[64,128]{1,0:T(8,128)(2,1)S(1)}, bf16[64,128]{1,0:T(8,128)(2,1)}, u32[]{:S(2)}) copy-start(bf16[64,128]{1,0:T(8,128)(2,1)} %constant.47.grad_table) | copy-start | bytes 49156
  130.1 12.8 %copy-start.8 = (bf16[64,128]{1,0:T(8,128)(2,1)S(1)}, bf16[64,128]{1,0:T(8,128)(2,1)}, u32[]{:S(2)}) copy-start(bf16[64,128]{1,0:T(8,128)(2,1)} %constant.45.output_table) | copy-start | bytes 49156
  143.0 3.4 %copy-start = (bf16[8,128,32,64]{3,2,1,0:T(8,128)(2,1)S(1)}, bf16[8,128,32,64]{3,2,1,0:T(8,128)(2,1)}, u32[]{:S(2)}) copy-start(bf16[8,128,32,64]{3,2,1,0:T(8,128)(2,1)} %copy.72) | copy-start | bytes 12582916
